TPU v7x, 32 devices: a whole 2x2x4 slice. The times are simulated.
32 devices in a mesh: band: 8 (over y, x, core), ga: 4 (over z).
Axes of the slice: x: 2, y: 2, z: 4, core: 2. Of those that a mesh axis runs over, the one named last changes fastest.
Arguments:
- coeffs: float32 [1024, 16384], P('band', 'ga'), may hold values from -90 to 90, as said below
Outputs:
- orthonormal: float32 [1024, 16384], P('band', 'ga')
Inputs may be any that keep to these rules, and one draw needn't show every extreme that they name: `coeffs`: bands are linearly independent.
All inputs are finite; a program needn't handle non-finite values.
Results may differ from a plain program's by a relative error of at most 0.00029.
Values sent between devices are 32-bit elements; how exact they have to be, the bound alone decides.
No kernel may reach another device: no remote copies, remote signals or barrier semaphores. Data moves between devices by JAX's collectives and lax.ppermute only.
A program may use at most 128 MiB of HBM per device.

v0:
```python
import jax
import jax.numpy as jnp
from jax import lax
from jax.sharding import PartitionSpec as P


def local(coeffs):
    band_rows, width = coeffs.shape
    columns_all = width * lax.axis_size("ga")
    gathered = lax.all_gather(coeffs, "band", axis=0, tiled=True)
    partial_value = (
        jnp.dot(
            coeffs, gathered.T, precision=lax.Precision.HIGHEST, preferred_element_type=jnp.float32
        )
        / columns_all
    )
    summed = lax.psum(partial_value, "ga")
    margin = lax.all_gather(summed, "band", axis=0, tiled=True)
    factor = jnp.linalg.cholesky(margin)
    order = factor.shape[0]
    start = lax.axis_index("band") * band_rows
    row_ids = lax.broadcasted_iota(jnp.int32, (order, band_rows), 0)
    col_ids = lax.broadcasted_iota(jnp.int32, (order, band_rows), 1)
    selector = jnp.where(row_ids == col_ids + start, 1.0, 0.0).astype(jnp.float32)
    solved = lax.linalg.triangular_solve(
        factor, selector, left_side=True, lower=True, transpose_a=True
    )
    own_rows = solved.T
    return jnp.dot(
        own_rows, gathered, precision=lax.Precision.HIGHEST, preferred_element_type=jnp.float32
    )


def solution(mesh):
    return jax.shard_map(
        local,
        mesh=mesh,
        in_specs=(P("band", "ga"),),
        out_specs=P("band", "ga"),
        check_vma=False,
    )
```

profile of v0, /device:TPU:0, one launch (start us, length us, event | category | flops | bytes accessed | tf_op | source)
XLA Modules:
  0.0 551.7 jit_solution(12576500978800521519)
XLA Ops:
  7.3 94.5 %all-gather.3.cloned.1.call-done = f32[1024,4096]{1,0:T(8,128)} async-done(((f32[128,4096]{1,0:T(8,128)}), f32[1024,4096]{1,0:T(8,128)}) %all-gather.3.cloned.1.call-update) | async-done | bytes 16777232 | tf_op jit(solution)/shard_map/all_gather | solution.py:10
  101.8 16.9 %convolution_multiply_fusion = f32[128,1024]{0,1:T(8,128)} fusion(f32[128,4096]{1,0:T(8,128)S(1)} %copy-done, f32[1024,4096]{1,0:T(8,128)} %all-gather.3.cloned.1.call-done), kind=kOutput, calls=%fused_computation.7 | convolution fusion | flops 6442582016 | bytes 19398656 | tf_op jit(solution)/shard_map/dot_general | solution.py:12
  118.8 38.4 %all-reduce.3.cloned.1.call-done = f32[128,1024]{0,1:T(8,128)} async-done(((f32[128,1024]{0,1:T(8,128)}), f32[128,1024]{0,1:T(8,128)}) %all-reduce.3.cloned.1.call-update) | async-done | bytes 524304 | tf_op jit(solution)/shard_map/psum | solution.py:17
  157.3 39.2 %all-gather.5.cloned.1.call-done = f32[1024,1024]{0,1:T(8,128)} async-done(((f32[128,1024]{0,1:T(8,128)}), f32[1024,1024]{0,1:T(8,128)}) %all-gather.5.cloned.1.call-update) | async-done | bytes 4194320 | tf_op jit(solution)/shard_map/all_gather | solution.py:18
  196.6 5.8 %copy.3 = f32[1024,1024]{1,0:T(8,128)} copy(f32[1024,1024]{0,1:T(8,128)} %all-gather.5.cloned.1.call-done) | data formatting | bytes 8388608 | tf_op jit(solution)/shard_map/all_gather | solution.py:18
  202.4 4.4 fusion
  208.8 11.7 %cholesky.223 = f32[128,128]{1,0:T(8,128)S(1)} custom-call(f32[128,128]{1,0:T(8,128)S(1)} %cholesky.580), custom_call_target="Cholesky" | custom-call | tf_op jit(solution)/shard_map/jit(cholesky)/cholesky | solution.py:19
  220.5 9.8 %custom-call.62 = f32[1,128,128]{1,2,0:T(8,128)S(1)} custom-call(f32[1,128,128]{2,1,0:T(8,128)S(1)} %get-tuple-element.44), custom_call_target="InvertDiagBlocksLowerTriangular" | custom-call | tf_op jit(solution)/shard_map/jit(cholesky)/cholesky | solution.py:19
  230.4 2.5 cholesky.255
  232.9 2.3 constant_dynamic-update-slice_fusion.32
  236.8 11.9 %cholesky.244 = f32[128,128]{1,0:T(8,128)S(1)} custom-call(f32[128,128]{1,0:T(8,128)S(1)} %cholesky.584), custom_call_target="Cholesky" | custom-call | tf_op jit(solution)/shard_map/jit(cholesky)/cholesky | solution.py:19
  249.3 9.8 %custom-call.63 = f32[1,128,128]{1,2,0:T(8,128)S(1)} custom-call(f32[1,128,128]{2,1,0:T(8,128)S(1)} %get-tuple-element.41), custom_call_target="InvertDiagBlocksLowerTriangular" | custom-call | tf_op jit(solution)/shard_map/jit(cholesky)/cholesky | solution.py:19
  262.4 11.7 %cholesky.468 = f32[128,128]{1,0:T(8,128)S(1)} custom-call(f32[128,128]{1,0:T(8,128)S(1)} %cholesky.589), custom_call_target="Cholesky" | custom-call | tf_op jit(solution)/shard_map/jit(cholesky)/cholesky | solution.py:19
  275.4 9.8 %custom-call.64 = f32[1,128,128]{1,2,0:T(8,128)S(1)} custom-call(f32[1,128,128]{2,1,0:T(8,128)S(1)} %get-tuple-element.38), custom_call_target="InvertDiagBlocksLowerTriangular" | custom-call | tf_op jit(solution)/shard_map/jit(cholesky)/cholesky | solution.py:19
  286.4 2.3 convolution_subtract_fusion.2
  288.8 11.9 %cholesky.487 = f32[128,128]{1,0:T(8,128)S(1)} custom-call(f32[128,128]{1,0:T(8,128)S(1)} %cholesky.594), custom_call_target="Cholesky" | custom-call | tf_op jit(solution)/shard_map/jit(cholesky)/cholesky | solution.py:19
  301.9 9.8 %custom-call.65 = f32[1,128,128]{1,2,0:T(8,128)S(1)} custom-call(f32[1,128,128]{2,1,0:T(8,128)S(1)} %get-tuple-element.35), custom_call_target="InvertDiagBlocksLowerTriangular" | custom-call | tf_op jit(solution)/shard_map/jit(cholesky)/cholesky | solution.py:19
  312.9 2.4 convolution_subtract_fusion.3
  315.3 11.7 %cholesky.506 = f32[128,128]{1,0:T(8,128)S(1)} custom-call(f32[128,128]{1,0:T(8,128)S(1)} %cholesky.599), custom_call_target="Cholesky" | custom-call | tf_op jit(solution)/shard_map/jit(cholesky)/cholesky | solution.py:19
  328.3 10.2 %custom-call.66 = f32[1,128,128]{1,2,0:T(8,128)S(1)} custom-call(f32[1,128,128]{2,1,0:T(8,128)S(1)} %get-tuple-element.32), custom_call_target="InvertDiagBlocksLowerTriangular" | custom-call | tf_op jit(solution)/shard_map/jit(cholesky)/cholesky | solution.py:19
  339.5 2.3 convolution_subtract_fusion.4
  341.8 11.7 %cholesky.526 = f32[128,128]{1,0:T(8,128)S(1)} custom-call(f32[128,128]{1,0:T(8,128)S(1)} %cholesky.604), custom_call_target="Cholesky" | custom-call | tf_op jit(solution)/shard_map/jit(cholesky)/cholesky | solution.py:19
  354.8 9.8 %custom-call.67 = f32[1,128,128]{1,2,0:T(8,128)S(1)} custom-call(f32[1,128,128]{2,1,0:T(8,128)S(1)} %get-tuple-element.29), custom_call_target="InvertDiagBlocksLowerTriangular" | custom-call | tf_op jit(solution)/shard_map/jit(cholesky)/cholesky | solution.py:19
  367.6 11.9 %cholesky.546 = f32[128,128]{1,0:T(8,128)S(1)} custom-call(f32[128,128]{1,0:T(8,128)S(1)} %cholesky.609), custom_call_target="Cholesky" | custom-call | tf_op jit(solution)/shard_map/jit(cholesky)/cholesky | solution.py:19
  380.8 9.8 %custom-call.68 = f32[1,128,128]{1,2,0:T(8,128)S(1)} custom-call(f32[1,128,128]{2,1,0:T(8,128)S(1)} %get-tuple-element.26), custom_call_target="InvertDiagBlocksLowerTriangular" | custom-call | tf_op jit(solution)/shard_map/jit(cholesky)/cholesky | solution.py:19
  393.2 11.7 %cholesky.564 = f32[128,128]{1,0:T(8,128)S(1)} custom-call(f32[128,128]{1,0:T(8,128)S(1)} %convolution_subtract_fusion.11), custom_call_target="Cholesky" | custom-call | tf_op jit(solution)/shard_map/jit(cholesky)/cholesky | solution.py:19
  411.8 4.8 select_select_fusion
  416.6 22.9 %while.1 = (s32[]{:T(128)}, f32[1024,1024]{1,0:T(8,128)}, s32[8,2]{0,1:T(2,128)S(1)}, f32[8,128,128]{2,1,0:T(8,128)S(1)}, s32[]{:T(128)}) while((s32[]{:T(128)}, f32[1024,1024]{1,0:T(8,128)}, s32[8,2]{0,1:T(2,128)S(1)}, f32[8,128,128]{2,1,0:T(8,128)S(1)}, s32[]{:T(128)}) %tuple.38), condition=%wide.while_cond, body=%wide.while_body.sunk | while | flops 2 | bytes 131181 | solution.py:25
  417.3 2.2 bitcast_dynamic-update-slice_fusion.2
  420.1 2.2 bitcast_dynamic-update-slice_fusion.2
  439.5 78.8 %custom-call.69 = f32[8,128,128]{1,2,0:T(8,128)S(1)} custom-call(f32[8,128,128]{2,1,0:T(8,128)S(1)} %get-tuple-element.12), custom_call_target="InvertDiagBlocksLowerTriangular" | custom-call | tf_op jit(solution)/shard_map/triangular_solve | solution.py:25
  531.2 13.7 %fusion.63 = f32[128,4096]{1,0:T(8,128)} fusion(f32[1024,128]{1,0:T(8,128)S(1)} %constant_dynamic-update-slice_fusion.18, f32[1024,4096]{1,0:T(8,128)} %all-gather.3.cloned.1.call-done), kind=kOutput, calls=%fused_computation.159 | convolution fusion | flops 6442450944 | bytes 19398656 | tf_op jit(solution)/shard_map/dot_general | solution.py:29
  (106 shorter events, 56.7 us)
Async XLA Ops:
  6.5 95.3 %copy-start = (f32[128,4096]{1,0:T(8,128)S(1)}, f32[128,4096]{1,0:T(8,128)}, u32[]{:S(2)}) copy-start(f32[128,4096]{1,0:T(8,128)} %param.1) | copy-start | bytes 6291460
  6.5 95.3 %all-gather.3.cloned.1.call-start = ((), (), s32[]{:S(2)}) async-start(), calls=%async_computation | async-start | bytes 18874368 | tf_op jit(solution)/shard_map/all_gather | solution.py:10
  7.3 150.0 %all-reduce.3.cloned.1.call-start = ((), (), s32[]{:S(2)}) async-start(), calls=%async_computation.1 | async-start | bytes 1048576 | tf_op jit(solution)/shard_map/psum | solution.py:17
  118.8 77.8 %all-gather.5.cloned.1.call-start = ((), (), s32[]{:S(2)}) async-start(), calls=%async_computation.2 | async-start | bytes 4718592 | tf_op jit(solution)/shard_map/all_gather | solution.py:18
  206.9 1.9 copy-start.1
Sparse Core Ops, SparseCore 0:
  9.2 92.5 all-gather.2
  118.9 38.2 all-reduce.2
  159.1 37.4 all-gather.4
where the time goes:
time: 555 us; the launch traced here: 552 us
  other arithmetic  260 us (47%)
  waiting for transfers between devices  173 us (31%)
  matrix products  66.2 us (12%)
  local copies, waits for them, and re-layouts  33.2 us (6%)
  between operations  18.8 us (3%)
    another operation x30, other arithmetic, local(): factor = jnp.linalg.cholesky(margin)  172 us
    all_gather x1, waiting for transfers between devices, local(): gathered = lax.all_gather(coeffs, 'band', axis=0, tiled=True)  94.5 us
    another operation x3, other arithmetic, local(): lax.linalg.triangular_solve(factor, selector, left_side=True, lower=True,...  83.6 us
    all_gather x1, waiting for transfers between devices, local(): margin = lax.all_gather(summed, 'band', axis=0, tiled=True)  39.2 us
    psum x1, waiting for transfers between devices, local(): summed = lax.psum(partial_value, 'ga')  38.4 us
    another operation x14, matrix products, local(): factor = jnp.linalg.cholesky(margin)  23.1 us
    another operation x24, local copies, waits for them, and re-layouts  22.7 us
    dot_general x1, matrix products, local(): jnp.dot(coeffs, gathered.T, precision=lax.Precision.HIGHEST, preferred_el...  16.9 us
  transfers between devices with their start and end apart: 3, of which 3 were waited for; matrix products, arithmetic and copies ran while one was open for 0% of the time, Pallas kernels for 0%

commit v1 on v0

v1 whole, which is shorter than its diff:
```python
import functools

import jax
import jax.numpy as jnp
from jax import lax
from jax.experimental import pallas as pl
from jax.experimental.pallas import tpu as pltpu
from jax.sharding import PartitionSpec as P

BLOCK = 128
STRIP = 8
NN = (((1,), (0,)), ((), ()))
NT = (((1,), (1,)), ((), ()))


def halves(x):
    high = x.astype(jnp.bfloat16)
    return high, (x - high.astype(jnp.float32)).astype(jnp.bfloat16)


def left3(x):
    high, low = halves(x)
    return jnp.concatenate([high, low, high], axis=1)


def right3(x):
    high, low = halves(x)
    return jnp.concatenate([high, high, low], axis=0)


def right3t(x):
    high, low = halves(x)
    return jnp.concatenate([high, high, low], axis=1)


def mm(a, b, dims=NN):
    return lax.dot_general(a, b, dims, preferred_element_type=jnp.float32)


def leaf(strips):
    strips = list(strips)
    count = len(strips)
    shape = strips[0].shape
    lane = lax.broadcasted_iota(jnp.int32, shape, 1)
    sub = lax.broadcasted_iota(jnp.int32, shape, 0)
    for s in range(count):
        base = STRIP * s
        rows = [jnp.broadcast_to(strips[s][q : q + 1, :], shape) for q in range(STRIP)]
        piv = [
            [
                jnp.broadcast_to(rows[a][:, base + b : base + b + 1], shape) if b >= a else None
                for b in range(STRIP)
            ]
            for a in range(STRIP)
        ]
        panel = (lane >= base) & (lane < base + STRIP)
        rows = [
            jnp.where(panel, jnp.where(lane == base + q, 1.0, 0.0), rows[q]) for q in range(STRIP)
        ]
        mult = [[None] * STRIP for _ in range(STRIP)]
        done = [None] * STRIP
        gain = [None] * STRIP
        for q in range(STRIP):
            inv = 1.0 / piv[q][q]
            for a in range(q + 1, STRIP):
                mult[a][q] = piv[q][a] * inv
            for a in range(q + 1, STRIP):
                for b in range(a, STRIP):
                    piv[a][b] = piv[a][b] - mult[a][q] * piv[q][b]
                rows[a] = rows[a] - mult[a][q] * rows[q]
            gain[q] = rows[q] * inv
            done[q] = rows[q] * lax.rsqrt(piv[q][q])
        for q in range(STRIP - 1, 0, -1):
            for a in range(q):
                gain[a] = gain[a] - mult[q][a] * gain[q]
        for t in range(s + 1, count):
            terms = [
                jnp.broadcast_to(strips[t][:, base + q : base + q + 1], shape) * gain[q]
                for q in range(STRIP)
            ]
            while len(terms) > 1:
                terms = [terms[i] + terms[i + 1] for i in range(0, len(terms), 2)]
            strips[t] = jnp.where(panel, 0.0, strips[t]) - terms[0]
        new = done[0]
        for q in range(1, STRIP):
            new = jnp.where(sub == q, done[q], new)
        strips[s] = new
    return [jnp.where(lane <= sub + STRIP * s, strips[s], 0.0) for s in range(count)]


def factor_kernel(order, m_ref, x_ref, v_ref, r_ref):
    wide = 2 * BLOCK
    for lo in range(0, order, BLOCK):
        src = m_ref if lo == 0 else x_ref
        hi = lo + BLOCK
        w = jnp.concatenate(leaf([src[lo + s : lo + s + STRIP, lo:hi] for s in range(0, BLOCK, STRIP)]), axis=0)
        w_left, w_rightt = left3(w), right3t(w)
        r_ref[:, lo:hi] = right3(w)
        if hi < order:
            v_ref[: order - hi, :] = left3(mm(left3(src[hi:, lo:hi]), w_rightt, NT))
        for c in range(0, order, wide):
            parts = [(c, c + wide)] if not c <= lo < c + wide else [(c, c + BLOCK), (c + BLOCK, c + wide)]
            for a, b in parts:
                if a == lo:
                    continue
                t = mm(w_left, right3(src[lo:hi, a:b]))
                x_ref[lo:hi, a:b] = t if a < lo else jnp.zeros_like(t)
                r_ref[:, a:b] = right3(t)
        x_ref[lo:hi, lo:hi] = w
        if hi < order:
            for c in range(0, order, wide):
                t = mm(v_ref[: order - hi, :], r_ref[:, c : c + wide])
                if not c <= lo < c + wide:
                    x_ref[hi:, c : c + wide] = src[hi:, c : c + wide] - t
                else:
                    for d in (c, c + BLOCK):
                        part = t[:, d - c : d - c + BLOCK]
                        x_ref[hi:, d : d + BLOCK] = -part if d == lo else src[hi:, d : d + BLOCK] - part


def inverse_factor(margin):
    order = margin.shape[0]
    return pl.pallas_call(
        functools.partial(factor_kernel, order),
        out_shape=jax.ShapeDtypeStruct((order, order), jnp.float32),
        in_specs=[pl.BlockSpec(memory_space=pltpu.VMEM)],
        out_specs=pl.BlockSpec(memory_space=pltpu.VMEM),
        scratch_shapes=[
            pltpu.VMEM((order - BLOCK, 3 * BLOCK), jnp.bfloat16),
            pltpu.VMEM((3 * BLOCK, order), jnp.bfloat16),
        ],
        compiler_params=pltpu.CompilerParams(vmem_limit_bytes=40 * 2**20),
    )(margin)


def local(coeffs):
    band_rows, width = coeffs.shape
    columns_all = width * lax.axis_size("ga")
    gathered = lax.all_gather(coeffs, "band", axis=0, tiled=True)
    partial_value = (
        jnp.dot(
            coeffs, gathered.T, precision=lax.Precision.HIGH, preferred_element_type=jnp.float32
        )
        / columns_all
    )
    summed = lax.psum(partial_value, "ga")
    margin = lax.all_gather(summed, "band", axis=0, tiled=True)
    inverse = inverse_factor(margin)
    own_rows = lax.dynamic_slice_in_dim(inverse, lax.axis_index("band") * band_rows, band_rows, 0)
    return jnp.dot(
        own_rows, gathered, precision=lax.Precision.HIGH, preferred_element_type=jnp.float32
    )


def solution(mesh):
    return jax.shard_map(
        local,
        mesh=mesh,
        in_specs=(P("band", "ga"),),
        out_specs=P("band", "ga"),
        check_vma=False,
    )
```

time: 555 us -> 266 us (0.48)
  other arithmetic: 260 us -> 0 us
  Pallas kernels: 0 us -> 46.9 us
  matrix products: 66.2 us -> 26 us
  local copies, waits for them, and re-layouts: 33.2 us -> 2.19 us
    another operation x33 -> x0, other arithmetic: 256 us -> none  [the longest x30 172 us: local(): factor = jnp.linalg.cholesky(margin)]
    pallas_call x0 -> x1, Pallas kernels: none -> 46.9 us  [inverse_factor(): pl.pallas_call(functools.partial(factor_kernel, order), out_shape=jax.Sha...]
    another operation x29 -> x0, matrix products: 35.5 us -> none  [the longest x14 23.1 us: local(): factor = jnp.linalg.cholesky(margin)]
    another operation x37 -> x0, local copies, waits for them, and re-layouts: 25.3 us -> none
    all_gather x1 -> x0, local copies, waits for them, and re-layouts: 5.85 us -> none  [local(): margin = lax.all_gather(summed, 'band', axis=0, tiled=True)]
where the time goes in v1:
time: 266 us; the launch traced here: 261 us
  waiting for transfers between devices  172 us (65%)
  Pallas kernels  46.9 us (18%)
  matrix products  26 us (10%)
  between operations  13.6 us (5%)
    all_gather x1, waiting for transfers between devices, local(): gathered = lax.all_gather(coeffs, 'band', axis=0, tiled=True)  94.5 us
    pallas_call x1, Pallas kernels, inverse_factor(): pl.pallas_call(functools.partial(factor_kernel, order), out_shape=jax.Sha...  46.9 us
    all_gather x1, waiting for transfers between devices, local(): margin = lax.all_gather(summed, 'band', axis=0, tiled=True)  38.6 us
    psum x1, waiting for transfers between devices, local(): summed = lax.psum(partial_value, 'ga')  38.2 us
    dot_general x1, matrix products, local(): jnp.dot(coeffs, gathered.T, precision=lax.Precision.HIGH, preferred_eleme...  15.5 us
    dot_general x1, matrix products, local(): jnp.dot(own_rows, gathered, precision=lax.Precision.HIGH, preferred_eleme...  10.4 us
  transfers between devices with their start and end apart: 3, of which 3 were waited for; matrix products, arithmetic and copies ran while one was open for 0% of the time, Pallas kernels for 0%

profile of v1, /device:TPU:0, one launch (start us, length us, event | category | flops | bytes accessed | tf_op | source)
XLA Modules:
  0.0 261.0 jit_solution(546346335599397817)
XLA Ops:
  6.5 0.0 all-gather.3.cloned.1.call-start
  6.5 0.7 all-gather.3.cloned.1.call-update
  7.3 0.0 all-reduce.2.cloned.1.call-start
  7.3 94.5 %all-gather.3.cloned.1.call-done = f32[1024,4096]{1,0:T(8,128)} async-done(((f32[128,4096]{1,0:T(8,128)}), f32[1024,4096]{1,0:T(8,128)}) %all-gather.3.cloned.1.call-update) | async-done | bytes 16777232 | tf_op jit(solution)/shard_map/all_gather | solution.py:139
  101.8 15.5 %convolution_multiply_fusion = f32[128,1024]{1,0:T(8,128)} fusion(f32[128,4096]{1,0:T(8,128)} %param.1, f32[1024,4096]{1,0:T(8,128)} %all-gather.3.cloned.1.call-done), kind=kOutput, calls=%fused_computation | convolution fusion | flops 3221356544 | bytes 19398656 | tf_op jit(solution)/shard_map/dot_general | solution.py:141
  117.4 0.0 all-reduce.2.cloned.1.call-update
  117.4 0.2 all-gather.5.cloned.1.call-start
  117.6 38.2 %all-reduce.2.cloned.1.call-done = f32[128,1024]{1,0:T(8,128)} async-done(((f32[128,1024]{1,0:T(8,128)}), f32[128,1024]{1,0:T(8,128)}) %all-reduce.2.cloned.1.call-update) | async-done | bytes 524304 | tf_op jit(solution)/shard_map/psum | solution.py:146
  155.9 0.0 all-gather.5.cloned.1.call-update
  155.9 38.6 %all-gather.5.cloned.1.call-done.m_ref = f32[1024,1024]{1,0:T(8,128)} async-done(((f32[128,1024]{1,0:T(8,128)}), f32[1024,1024]{1,0:T(8,128)}) %all-gather.5.cloned.1.call-update) | async-done | bytes 4194320 | tf_op jit(solution)/shard_map/all_gather | solution.py:147
  194.5 0.0 copy-start
  194.5 2.2 copy-done
  196.7 46.9 %shard_map.17 = f32[1024,1024]{1,0:T(8,128)S(1)} custom-call(f32[1024,1024]{1,0:T(8,128)S(1)} %copy-done), custom_call_target="tpu_custom_call" | custom-call | tf_op jit(solution)/shard_map/pallas_call | solution.py:123
  243.6 10.4 %fusion = f32[128,4096]{1,0:T(8,128)} fusion(f32[1024,4096]{1,0:T(8,128)} %all-gather.3.cloned.1.call-done, f32[1024,1024]{1,0:T(8,128)S(1)} %shard_map.17, s32[]{:T(128)S(6)} %select_n.3), kind=kOutput, calls=%fused_computation.1 | convolution fusion | flops 3221225472 | bytes 19398660 | tf_op jit(solution)/shard_map/dot_general | solution.py:150
Async XLA Ops:
  6.5 95.3 %all-gather.3.cloned.1.call-start = ((), (), s32[]{:S(2)}) async-start(), calls=%async_computation | async-start | bytes 18874368 | tf_op jit(solution)/shard_map/all_gather | solution.py:139
  7.3 148.6 %all-reduce.2.cloned.1.call-start = ((), (), s32[]{:S(2)}) async-start(), calls=%async_computation.1 | async-start | bytes 1048576 | tf_op jit(solution)/shard_map/psum | solution.py:146
  117.4 77.1 %all-gather.5.cloned.1.call-start = ((), (), s32[]{:S(2)}) async-start(), calls=%async_computation.2 | async-start | bytes 4718592 | tf_op jit(solution)/shard_map/all_gather | solution.py:147
  194.5 2.2 copy-start
Sparse Core Ops, SparseCore 0:
  9.2 92.5 all-gather.2
  117.5 38.2 all-reduce.1
  157.8 36.6 all-gather.4
